TPU v7x, 32 devices: a whole 2x2x4 slice. The times are simulated.
32 devices in a mesh: region: 4 (over x, core), blk: 8 (over z, y).
Axes of the slice: x: 2, y: 2, z: 4, core: 2. Of those that a mesh axis runs over, the one named last changes fastest.
Arguments:
- velocity: float32 [3, 64, 256, 256], P(None, 'region', 'blk'), may hold values from -5 to 5
- viscosity: float32 [64, 256, 256], P('region', 'blk'), may hold values from 0.02 to 0.1
- match_cell: int32 [32768], P(('region', 'blk')), may hold values from 0 to 131071
- wall_cell: int32 [32768], P(('region', 'blk')), may hold values from 0 to 131071
- match_dest: int32 [32768, 1], P(('region', 'blk')), may hold values from 0 to 31; in each aligned block of 1024 rows (0 to 1023, 1024 to 2047, ...) at most 64 rows name the same one
- match_count: int32 [32], P(('region', 'blk')), may hold values from 1 to 1024, 26214 in all
- wall_geom: float32 [4, 65536], P(None, ('region', 'blk')), may hold values from -1 to 1, as said below
Outputs:
- advanced: float32 [3, 64, 256, 256], P(None, 'region', 'blk')
- wall_log_stress: float32 [32768], P(('region', 'blk'))
Inputs may be any that keep to these rules, and one draw needn't show every extreme that they name: `match_dest`: among the 1024 rows of one device at most 64 name the same owner, and some device reaches 64. The first match_count rows of a device's matching points are live; some device has all 1024 live. `match_cell`: local cell index of the device's 16 x 32 x 256 cells. `wall_cell`: local cell index of the device's 16 x 32 x 256 cells. `wall_geom`: row 0 lies in 0.02 to 0.3; rows 1 to 3 have magnitudes 0.3 to 1.
All inputs are finite; a program needn't handle non-finite values.
Results may differ from a plain program's by a relative error of at most 0.0003.
Values sent between devices are 32-bit elements; how exact they have to be, the bound alone decides.
A program may use at most 192 MiB of HBM per device.

v0:
```python
import functools

import jax
import jax.numpy as jnp
from jax import lax
from jax.experimental import pallas as pl
from jax.experimental.pallas import tpu as pltpu
from jax.sharding import PartitionSpec as P

NEWTON = 2
KAPPA = 0.41
DAMPING = 26.0
NU_WALL = 0.0002
WALL_DY = 0.0005
TIME_STEP = 0.1
SPEED_FLOOR = 0.5
GUESS_RATIO = 14.0
LEVELS = 32

MESH = pl.DeviceIdType.MESH
BF16 = jnp.bfloat16
F32 = jnp.float32


def split2(x):
    hi = x.astype(BF16)
    return hi, (x - hi.astype(F32)).astype(BF16)


def split3(x):
    hi = x.astype(BF16)
    rest = x - hi.astype(F32)
    mid = rest.astype(BF16)
    return hi, mid, (rest - mid.astype(F32)).astype(BF16)


def one_hot(index_row, count):
    rows = lax.broadcasted_iota(jnp.int32, (count, index_row.shape[1]), 0)
    return jnp.where(rows == index_row, 1.0, 0.0)


def kernel(
    n_region, n_blk, cap,
    v_hbm, visc_ref, mcell_ref, wcell_ref, dest_ref, count_ref, geom_ref,
    adv_ref, log_ref,
    w1, w2, force, geo, ysend, yrecv1, yrecv2,
    oh_match, oh_wall, k_match, k_wall, vsplit, wsplit, wgeo,
    load_sem, gsend, grecv, own_sem, hsend, hrecv,
):
    comps, nx, ny, nz = v_hbm.shape
    rows_n = nx * ny
    points = mcell_ref.shape[1]
    devices = n_region * n_blk
    r = lax.axis_index("region")
    b = lax.axis_index("blk")
    me = r * n_blk + b

    barrier = pltpu.get_barrier_semaphore()

    @pl.loop(0, devices)
    def _(d):
        @pl.when(d != me)
        def _():
            pl.semaphore_signal(barrier, inc=1, device_id=(d // n_blk, d % n_blk), device_id_type=MESH)

    load = pltpu.make_async_copy(v_hbm, w1.at[:, 2 : 2 + nx, 8 : 8 + ny, :], load_sem)
    load.start()
    has = (r > 0, r < n_region - 1, b > 0, b < n_blk - 1)
    peers = ((r - 1, b), (r + 1, b), (r, b - 1), (r, b + 1))

    for w, yrecv in ((w1, yrecv1), (w2, yrecv2)):
        @pl.when(jnp.logical_not(has[0]))
        def _():
            w[:, 0:2, 8 : 8 + ny, :] = jnp.zeros((comps, 2, ny, nz), F32)

        @pl.when(jnp.logical_not(has[1]))
        def _():
            w[:, nx + 2 : nx + 4, 8 : 8 + ny, :] = jnp.zeros((comps, 2, ny, nz), F32)

        @pl.when(jnp.logical_not(has[2]))
        def _():
            yrecv[0] = jnp.zeros((comps, nx, 2, nz), F32)

        @pl.when(jnp.logical_not(has[3]))
        def _():
            yrecv[1] = jnp.zeros((comps, nx, 2, nz), F32)

    pl.semaphore_wait(barrier, devices - 1)

    def geo_copy(d):
        at = pl.multiple_of((d * cap) // 128 * 128, 128)
        return pltpu.make_async_remote_copy(
            src_ref=geom_ref.at[:, pl.ds(at, 128)],
            dst_ref=geo.at[me],
            send_sem=gsend.at[d],
            recv_sem=grecv.at[me],
            device_id=(d // n_blk, d % n_blk),
            device_id_type=MESH,
        )

    @pl.loop(0, devices)
    def _(d):
        @pl.when(d != me)
        def _():
            geo_copy(d).start()

    my_at = pl.multiple_of((me * cap) // 128 * 128, 128)
    own = pltpu.make_async_copy(geom_ref.at[:, pl.ds(my_at, 128)], geo.at[me], own_sem)
    own.start()

    def halo_copies(section, w, yrecv, xsource):
        out = []
        for side in range(4):
            if side == 0:
                src, dst = xsource(0), w.at[:, nx + 2 : nx + 4, 8 : 8 + ny, :]
            elif side == 1:
                src, dst = xsource(nx - 2), w.at[:, 0:2, 8 : 8 + ny, :]
            elif side == 2:
                src, dst = ysend.at[section, 0], yrecv.at[1]
            else:
                src, dst = ysend.at[section, 1], yrecv.at[0]
            out.append(
                pltpu.make_async_remote_copy(
                    src_ref=src, dst_ref=dst,
                    send_sem=hsend.at[section, side], recv_sem=hrecv.at[section, side],
                    device_id=peers[side], device_id_type=MESH,
                )
            )
        return out

    halo1 = halo_copies(0, w1, yrecv1, lambda i: v_hbm.at[:, i : i + 2])
    halo2 = halo_copies(1, w2, yrecv2, lambda i: w2.at[:, i + 2 : i + 4, 8 : 8 + ny, :])

    def start(copies, sides):
        for side in sides:
            pl.when(has[side])(copies[side].start)

    def finish(copies):
        for side in range(4):
            pl.when(has[side])(copies[side].wait_send)
            pl.when(has[side ^ 1])(copies[side].wait_recv)

    start(halo1, (0, 1))
    load.wait()

    def stage_y(section, w):
        @pl.loop(0, nx)
        def _(i):
            for c in range(comps):
                ysend[section, 0, c, i] = w[c, 2 + i, 8:10, :]
                ysend[section, 1, c, i] = w[c, 2 + i, 6 + ny : 8 + ny, :]

    stage_y(0, w1)
    start(halo1, (2, 3))

    mcell = mcell_ref[...]
    wcell = wcell_ref[...]
    live = lax.broadcasted_iota(jnp.int32, (1, points), 1) < count_ref[...]
    oh_match[...] = one_hot(mcell // nz, rows_n).astype(BF16)
    wall_rows = one_hot(wcell // nz, rows_n).astype(BF16)
    oh_wall[:, 0:points] = wall_rows
    oh_wall[:, points : 2 * points] = wall_rows
    k_match[...] = one_hot(mcell % nz, nz)
    k_wall[...] = one_hot(wcell % nz, nz).astype(BF16)

    own_mask = jnp.where(
        (lax.broadcasted_iota(jnp.int32, (devices, points), 0) == dest_ref[...]) & live, 1.0, 0.0
    )
    tri_row = lax.broadcasted_iota(jnp.int32, (128, 256), 0)
    tri_col = lax.broadcasted_iota(jnp.int32, (128, 256), 1)
    tri = jnp.where((tri_row < tri_col) | (tri_col >= 128), 1.0, 0.0).astype(BF16)
    before = jnp.zeros((devices, 128), F32)
    ranks = []
    for j in range(points // 128):
        part = own_mask[:, j * 128 : (j + 1) * 128]
        sums = jnp.dot(part.astype(BF16), tri, preferred_element_type=F32)
        ranks.append(jnp.sum(part * (sums[:, :128] + before), axis=0, keepdims=True))
        before = before + sums[:, 128:]
    rank = jnp.concatenate(ranks, axis=1).astype(jnp.int32)
    offset = me * cap - (me * cap) // 128 * 128
    rank_mask = one_hot(rank + offset, 128)
    own_bf = own_mask.astype(BF16)
    own3 = jnp.concatenate([own_bf, own_bf, own_bf], axis=0)

    def samples_of(w):
        got = []
        for c in range(comps):
            hi, lo = split2(w[c, 2 : 2 + nx, 8 : 8 + ny, :].reshape(rows_n, nz))
            acc = lax.dot_general(hi, oh_match[...], (((0,), (0,)), ((), ())), preferred_element_type=F32)
            acc = acc + lax.dot_general(lo, oh_match[...], (((0,), (0,)), ((), ())), preferred_element_type=F32)
            got.append(jnp.sum(acc * k_match[...], axis=0, keepdims=True))
        return got

    samples = samples_of(w1)

    own.wait()

    @pl.loop(0, devices)
    def _(d):
        @pl.when(d != me)
        def _():
            copy = pltpu.make_async_remote_copy(
                src_ref=geom_ref.at[:, pl.ds(my_at, 128)],
                dst_ref=geo.at[d],
                send_sem=gsend.at[d],
                recv_sem=grecv.at[d],
                device_id=(d // n_blk, d % n_blk),
                device_id_type=MESH,
            )
            copy.wait_send()
            copy.wait_recv()

    records = []
    for c in range(4):
        hi, mid, lo = split3(geo[:, c, :])
        three = jnp.concatenate([hi, mid, lo], axis=0)
        chosen = lax.dot_general(three, own3, (((0,), (0,)), ((), ())), preferred_element_type=F32)
        records.append(jnp.sum(chosen * rank_mask, axis=0, keepdims=True))
    distance = records[0]
    inv = 1.0 / jnp.sqrt(records[1] * records[1] + records[2] * records[2] + records[3] * records[3])
    normal = [records[1] * inv, records[2] * inv, records[3] * inv]

    level = lax.broadcasted_iota(jnp.int32, (LEVELS, 1), 0).astype(F32)
    last = LEVELS - 1.0
    eta = (level / last) * (level / last)
    above = jnp.minimum(level + 1.0, last) / last
    below = jnp.maximum(level - 1.0, 0.0) / last
    weight = 0.5 * (above * above - below * below)
    log_distance = jnp.log(distance)

    def wall_solve(got):
        along = got[0] * normal[0] + got[1] * normal[1] + got[2] * normal[2]
        tangent = [got[c] - along * normal[c] for c in range(comps)]
        speed = jnp.sqrt(tangent[0] * tangent[0] + tangent[1] * tangent[1] + tangent[2] * tangent[2])
        speed = jnp.maximum(speed, SPEED_FLOOR)
        target = jnp.log(speed)
        s = target - jnp.log(GUESS_RATIO)
        for _ in range(NEWTON):
            z = eta * (distance * jnp.exp(s))
            a = z * (1.0 / (NU_WALL * DAMPING))
            e = jnp.exp(-a)
            damp = 1.0 - e
            kzd = (KAPPA * z) * damp
            eddy = kzd * damp
            inv_den = 1.0 / (NU_WALL + eddy)
            f = weight * inv_den
            slope = (eddy + 2.0 * kzd * (e * a)) * inv_den
            total = jnp.sum(f, axis=0, keepdims=True)
            bend = jnp.sum(f * slope, axis=0, keepdims=True)
            value = log_distance + 2.0 * s + jnp.log(total) - target
            s = s - value / (2.0 - bend / total)
        factor = -jnp.exp(2.0 * s) / speed / WALL_DY
        return [jnp.where(live, factor * t, 0.0) for t in tangent], jnp.where(live, 2.0 * s, 0.0)

    def scatter(stress):
        for c in range(comps):
            hi, lo = split2(stress[c])
            wsplit[:, 0:points] = k_wall[...] * hi
            wsplit[:, points : 2 * points] = k_wall[...] * lo
            out = lax.dot_general(
                oh_wall[...], wsplit[...], (((1,), (1,)), ((), ())), preferred_element_type=F32
            )
            force[c] = out.reshape(nx, ny, nz)

    stress, _ = wall_solve(samples)
    scatter(stress)
    finish(halo1)

    lane = lax.broadcasted_iota(jnp.int32, (ny, nz), 1)

    def put_y(w, yrecv):
        @pl.loop(0, nx)
        def _(i):
            for c in range(comps):
                w[c, 2 + i, 6:8, :] = yrecv[0, c, i]
                w[c, 2 + i, 8 + ny : 10 + ny, :] = yrecv[1, c, i]

    def rate(w, i):
        nu = visc_ref[i]
        n16 = nu * (16.0 / 12.0)
        n1 = nu * (1.0 / 12.0)
        center = [w[c, 2 + i, 8 : 8 + ny, :] for c in range(comps)]
        acc = [force[c, i] - (7.5 * nu) * center[c] for c in range(comps)]
        for axis in range(3):
            g8 = center[axis] * (8.0 / 12.0)
            g1 = center[axis] * (1.0 / 12.0)
            p1, m1, p2, m2 = n16 - g8, n16 + g8, g1 - n1, -(g1 + n1)
            if axis == 2:
                p1 = jnp.where(lane < nz - 1, p1, 0.0)
                m1 = jnp.where(lane >= 1, m1, 0.0)
                p2 = jnp.where(lane < nz - 2, p2, 0.0)
                m2 = jnp.where(lane >= 2, m2, 0.0)
            for c in range(comps):
                if axis == 0:
                    near = [w[c, 2 + i + s, 8 : 8 + ny, :] for s in (1, -1, 2, -2)]
                elif axis == 1:
                    near = [w[c, 2 + i, 8 + s : 8 + s + ny, :] for s in (1, -1, 2, -2)]
                else:
                    near = [pltpu.roll(center[c], s % nz, 1) for s in (-1, 1, -2, 2)]
                acc[c] = acc[c] + ((p1 * near[0] + m1 * near[1]) + (p2 * near[2] + m2 * near[3]))
        return center, acc

    put_y(w1, yrecv1)

    @pl.loop(0, nx)
    def _(i):
        center, acc = rate(w1, i)
        for c in range(comps):
            w2[c, 2 + i, 8 : 8 + ny, :] = center[c] + TIME_STEP * acc[c]

    start(halo2, (0, 1))
    stage_y(1, w2)
    start(halo2, (2, 3))
    stress, logs = wall_solve(samples_of(w2))
    log_ref[...] = logs
    scatter(stress)
    finish(halo2)
    put_y(w2, yrecv2)

    @pl.loop(0, nx)
    def _(i):
        center, acc = rate(w2, i)
        for c in range(comps):
            v = w1[c, 2 + i, 8 : 8 + ny, :]
            adv_ref[c, i] = 0.5 * v + 0.5 * (center[c] + TIME_STEP * acc[c])


def local(n_region, n_blk, velocity, viscosity, match_cell, wall_cell, match_dest, match_count, wall_geom):
    comps, nx, ny, nz = velocity.shape
    points = match_cell.shape[0]
    devices = n_region * n_blk
    cap = wall_geom.shape[1] // devices
    vmem = pl.BlockSpec(memory_space=pltpu.VMEM)
    field = pltpu.VMEM((comps, nx + 4, ny + 16, nz), F32)
    advanced, log_stress = pl.pallas_call(
        functools.partial(kernel, n_region, n_blk, cap),
        out_shape=(
            jax.ShapeDtypeStruct((comps, nx, ny, nz), F32),
            jax.ShapeDtypeStruct((1, points), F32),
        ),
        in_specs=[pl.BlockSpec(memory_space=pl.ANY)] + [vmem] * 6,
        out_specs=(vmem, vmem),
        scratch_shapes=[
            field,
            field,
            pltpu.VMEM((comps, nx, ny, nz), F32),
            pltpu.VMEM((devices, 4, 128), F32),
            pltpu.VMEM((2, 2, comps, nx, 2, nz), F32),
            pltpu.VMEM((2, comps, nx, 2, nz), F32),
            pltpu.VMEM((2, comps, nx, 2, nz), F32),
            pltpu.VMEM((nx * ny, points), BF16),
            pltpu.VMEM((nx * ny, 2 * points), BF16),
            pltpu.VMEM((nz, points), F32),
            pltpu.VMEM((nz, points), BF16),
            pltpu.VMEM((16, 128), BF16),
            pltpu.VMEM((nz, 2 * points), BF16),
            pltpu.VMEM((8, 128), F32),
            pltpu.SemaphoreType.DMA,
            pltpu.SemaphoreType.DMA((devices,)),
            pltpu.SemaphoreType.DMA((devices,)),
            pltpu.SemaphoreType.DMA,
            pltpu.SemaphoreType.DMA((2, 4)),
            pltpu.SemaphoreType.DMA((2, 4)),
        ],
        compiler_params=pltpu.CompilerParams(
            collective_id=0, has_side_effects=True, vmem_limit_bytes=56 * 1024 * 1024
        ),
    )(
        velocity,
        viscosity,
        match_cell.reshape(1, points),
        wall_cell.reshape(1, points),
        match_dest.reshape(1, points),
        match_count.reshape(1, 1),
        wall_geom,
    )
    return advanced, log_stress.reshape(points)


def solution(mesh):
    placed = (
        P(None, "region", "blk", None),
        P("region", "blk", None),
        P(("region", "blk")),
        P(("region", "blk")),
        P(("region", "blk"), None),
        P(("region", "blk")),
        P(None, ("region", "blk")),
    )
    return jax.shard_map(
        functools.partial(local, mesh.shape["region"], mesh.shape["blk"]),
        mesh=mesh,
        in_specs=placed,
        out_specs=(P(None, "region", "blk", None), P(("region", "blk"))),
        check_vma=False,
    )
```

profile of v0, /device:TPU:0, one launch (start us, length us, event | category | flops | bytes accessed | tf_op | source)
XLA Modules:
  0.0 32.5 jit_solution(9232708827399754145)
XLA Ops:
  1.3 27.9 %shard_map.86 = (f32[3,16,32,256]{3,2,1,0:T(8,128)}, f32[1,1024]{1,0:T(1,128)}) custom-call(f32[3,16,32,256]{3,2,1,0:T(8,128)} %v_hbm.1, f32[16,32,256]{2,1,0:T(8,128)} %visc_ref.1, s32[1,1024]{1,0:T(1,128)} %bitcast.6, s32[1,1024]{1,0:T(1,128)} %bitcast.7, s32[1,1024]{1,0:T(1,128)} %bitcast.8, s32[1,1]{1,0:T(1,128)} %bitcast.5.count_ref, f32[4,2048]{1,0:T(4,128)} %geom_ref.1), custom_call_target="tpu_custom_call" | custom-call | tf_op jit(solution)/shard_map/pallas_call | solution.py:335
  29.2 0.0 copy-start
  29.2 2.7 %copy.12 = f32[3,16,32,256]{3,2,1,0:T(8,128)} copy(f32[3,16,32,256]{3,2,1,0:T(8,128)} %get-tuple-element.8) | data formatting | bytes 3145728
  31.9 0.0 copy-done
  31.9 0.6 %copy.13 = f32[1024]{0:T(1024)} copy(f32[1024]{0:T(1024)S(1)} %bitcast.9) | data formatting | bytes 8192
Async XLA Ops:
  29.2 2.7 %copy-start = (f32[1,1024]{1,0:T(1,128)S(1)}, f32[1,1024]{1,0:T(1,128)}, u32[]{:S(2)}) copy-start(f32[1,1024]{1,0:T(1,128)} %get-tuple-element.5) | copy-start | bytes 12292
where the time goes:
time: 32.7 us; the launch traced here: 32.5 us
  Pallas kernels  27.9 us (85%)
  local copies, waits for them, and re-layouts  3.33 us (10%)
  between operations  1.29 us (4%)
    pallas_call x1, Pallas kernels, local(): pl.pallas_call(functools.partial(kernel, n_region, n_blk, cap), out_shape...  27.9 us
    unnamed x4, local copies, waits for them, and re-layouts  3.33 us

commit v1 on v0

--- a/solution.py
+++ b/solution.py
@@ -41,11 +41,11 @@
 
 def kernel(
     n_region, n_blk, cap,
-    v_hbm, visc_ref, mcell_ref, wcell_ref, dest_ref, count_ref, geom_ref,
-    adv_ref, log_ref,
-    w1, w2, force, geo, ysend, yrecv1, yrecv2,
-    oh_match, oh_wall, k_match, k_wall, vsplit, wsplit, wgeo,
-    load_sem, gsend, grecv, own_sem, hsend, hrecv,
+    v_hbm, visc_hbm, mcell_ref, wcell_ref, dest_ref, count_ref, geom_ref,
+    adv_hbm, log_ref,
+    visc_ref, adv_buf, w1, w2, force, geo, ysend, yrecv1, yrecv2,
+    oh_match, oh_wall, k_match, k_wall, wsplit,
+    load_sem, visc_sem, out_sem, gsend, grecv, own_sem, hsend, hrecv,
 ):
     comps, nx, ny, nz = v_hbm.shape
     rows_n = nx * ny
@@ -65,6 +65,8 @@
 
     load = pltpu.make_async_copy(v_hbm, w1.at[:, 2 : 2 + nx, 8 : 8 + ny, :], load_sem)
     load.start()
+    load_visc = pltpu.make_async_copy(visc_hbm, visc_ref, visc_sem)
+    load_visc.start()
     has = (r > 0, r < n_region - 1, b > 0, b < n_blk - 1)
     peers = ((r - 1, b), (r + 1, b), (r, b - 1), (r, b + 1))
 
@@ -84,6 +86,35 @@
         @pl.when(jnp.logical_not(has[3]))
         def _():
             yrecv[1] = jnp.zeros((comps, nx, 2, nz), F32)
+
+    mcell = mcell_ref[...]
+    wcell = wcell_ref[...]
+    live = lax.broadcasted_iota(jnp.int32, (1, points), 1) < count_ref[...]
+    oh_match[...] = one_hot(mcell // nz, rows_n).astype(BF16)
+    wall_rows = one_hot(wcell // nz, rows_n).astype(BF16)
+    oh_wall[:, 0:points] = wall_rows
+    oh_wall[:, points : 2 * points] = wall_rows
+    k_match[...] = one_hot(mcell % nz, nz)
+    k_wall[...] = one_hot(wcell % nz, nz).astype(BF16)
+
+    own_mask = jnp.where(
+        (lax.broadcasted_iota(jnp.int32, (devices, points), 0) == dest_ref[...]) & live, 1.0, 0.0
+    )
+    tri_row = lax.broadcasted_iota(jnp.int32, (128, 256), 0)
+    tri_col = lax.broadcasted_iota(jnp.int32, (128, 256), 1)
+    tri = jnp.where((tri_row < tri_col) | (tri_col >= 128), 1.0, 0.0).astype(BF16)
+    before = jnp.zeros((devices, 128), F32)
+    ranks = []
+    for j in range(points // 128):
+        part = own_mask[:, j * 128 : (j + 1) * 128]
+        sums = jnp.dot(part.astype(BF16), tri, preferred_element_type=F32)
+        ranks.append(jnp.sum(part * (sums[:, :128] + before), axis=0, keepdims=True))
+        before = before + sums[:, 128:]
+    rank = jnp.concatenate(ranks, axis=1).astype(jnp.int32)
+    offset = me * cap - (me * cap) // 128 * 128
+    rank_mask = one_hot(rank + offset, 128)
+    own_bf = own_mask.astype(BF16)
+    own3 = jnp.concatenate([own_bf, own_bf, own_bf], axis=0)
 
     pl.semaphore_wait(barrier, devices - 1)
 
@@ -144,7 +175,7 @@
     load.wait()
 
     def stage_y(section, w):
-        @pl.loop(0, nx)
+        @pl.loop(0, nx, unroll=8)
         def _(i):
             for c in range(comps):
                 ysend[section, 0, c, i] = w[c, 2 + i, 8:10, :]
@@ -152,35 +183,6 @@
 
     stage_y(0, w1)
     start(halo1, (2, 3))
-
-    mcell = mcell_ref[...]
-    wcell = wcell_ref[...]
-    live = lax.broadcasted_iota(jnp.int32, (1, points), 1) < count_ref[...]
-    oh_match[...] = one_hot(mcell // nz, rows_n).astype(BF16)
-    wall_rows = one_hot(wcell // nz, rows_n).astype(BF16)
-    oh_wall[:, 0:points] = wall_rows
-    oh_wall[:, points : 2 * points] = wall_rows
-    k_match[...] = one_hot(mcell % nz, nz)
-    k_wall[...] = one_hot(wcell % nz, nz).astype(BF16)
-
-    own_mask = jnp.where(
-        (lax.broadcasted_iota(jnp.int32, (devices, points), 0) == dest_ref[...]) & live, 1.0, 0.0
-    )
-    tri_row = lax.broadcasted_iota(jnp.int32, (128, 256), 0)
-    tri_col = lax.broadcasted_iota(jnp.int32, (128, 256), 1)
-    tri = jnp.where((tri_row < tri_col) | (tri_col >= 128), 1.0, 0.0).astype(BF16)
-    before = jnp.zeros((devices, 128), F32)
-    ranks = []
-    for j in range(points // 128):
-        part = own_mask[:, j * 128 : (j + 1) * 128]
-        sums = jnp.dot(part.astype(BF16), tri, preferred_element_type=F32)
-        ranks.append(jnp.sum(part * (sums[:, :128] + before), axis=0, keepdims=True))
-        before = before + sums[:, 128:]
-    rank = jnp.concatenate(ranks, axis=1).astype(jnp.int32)
-    offset = me * cap - (me * cap) // 128 * 128
-    rank_mask = one_hot(rank + offset, 128)
-    own_bf = own_mask.astype(BF16)
-    own3 = jnp.concatenate([own_bf, own_bf, own_bf], axis=0)
 
     def samples_of(w):
         got = []
@@ -265,11 +267,12 @@
     stress, _ = wall_solve(samples)
     scatter(stress)
     finish(halo1)
+    load_visc.wait()
 
     lane = lax.broadcasted_iota(jnp.int32, (ny, nz), 1)
 
     def put_y(w, yrecv):
-        @pl.loop(0, nx)
+        @pl.loop(0, nx, unroll=8)
         def _(i):
             for c in range(comps):
                 w[c, 2 + i, 6:8, :] = yrecv[0, c, i]
@@ -312,7 +315,8 @@
     stage_y(1, w2)
     start(halo2, (2, 3))
     stress, logs = wall_solve(samples_of(w2))
-    log_ref[...] = logs
+    for j in range(points // 128):
+        log_ref[j : j + 1, :] = logs[:, j * 128 : (j + 1) * 128]
     scatter(stress)
     finish(halo2)
     put_y(w2, yrecv2)
@@ -322,7 +326,30 @@
         center, acc = rate(w2, i)
         for c in range(comps):
             v = w1[c, 2 + i, 8 : 8 + ny, :]
-            adv_ref[c, i] = 0.5 * v + 0.5 * (center[c] + TIME_STEP * acc[c])
+            adv_buf[c, i] = 0.5 * v + 0.5 * (center[c] + TIME_STEP * acc[c])
+        pltpu.make_async_copy(adv_buf.at[:, i], adv_hbm.at[:, i], out_sem).start()
+
+    pltpu.make_async_copy(adv_buf, adv_hbm, out_sem).wait()
+
+
+def hand_over(adv_in, log_in, adv_out, log_out, held, held_log, in_sems, out_sems):
+    comps, nx = adv_in.shape[:2]
+    step = nx // 4
+    last = 4 * comps
+    loads = [pltpu.make_async_copy(log_in, held_log, in_sems.at[last])]
+    stores = [pltpu.make_async_copy(held_log, log_out, out_sems.at[last])]
+    for c in range(comps):
+        for j in range(4):
+            part = (c, pl.ds(j * step, step))
+            loads.append(pltpu.make_async_copy(adv_in.at[part], held.at[part], in_sems.at[4 * c + j]))
+            stores.append(pltpu.make_async_copy(held.at[part], adv_out.at[part], out_sems.at[4 * c + j]))
+    for load in loads:
+        load.start()
+    for load, store in zip(loads, stores):
+        load.wait()
+        store.start()
+    for store in stores:
+        store.wait()
 
 
 def local(n_region, n_blk, velocity, viscosity, match_cell, wall_cell, match_dest, match_count, wall_geom):
@@ -331,16 +358,19 @@
     devices = n_region * n_blk
     cap = wall_geom.shape[1] // devices
     vmem = pl.BlockSpec(memory_space=pltpu.VMEM)
+    hbm = pl.BlockSpec(memory_space=pl.ANY)
     field = pltpu.VMEM((comps, nx + 4, ny + 16, nz), F32)
     advanced, log_stress = pl.pallas_call(
         functools.partial(kernel, n_region, n_blk, cap),
         out_shape=(
             jax.ShapeDtypeStruct((comps, nx, ny, nz), F32),
-            jax.ShapeDtypeStruct((1, points), F32),
+            jax.ShapeDtypeStruct((points // 128, 128), F32),
         ),
-        in_specs=[pl.BlockSpec(memory_space=pl.ANY)] + [vmem] * 6,
-        out_specs=(vmem, vmem),
+        in_specs=[hbm, hbm] + [vmem] * 5,
+        out_specs=(hbm, vmem),
         scratch_shapes=[
+            pltpu.VMEM((nx, ny, nz), F32),
+            pltpu.VMEM((comps, nx, ny, nz), F32),
             field,
             field,
             pltpu.VMEM((comps, nx, ny, nz), F32),
@@ -352,9 +382,9 @@
             pltpu.VMEM((nx * ny, 2 * points), BF16),
             pltpu.VMEM((nz, points), F32),
             pltpu.VMEM((nz, points), BF16),
-            pltpu.VMEM((16, 128), BF16),
             pltpu.VMEM((nz, 2 * points), BF16),
-            pltpu.VMEM((8, 128), F32),
+            pltpu.SemaphoreType.DMA,
+            pltpu.SemaphoreType.DMA,
             pltpu.SemaphoreType.DMA,
             pltpu.SemaphoreType.DMA((devices,)),
             pltpu.SemaphoreType.DMA((devices,)),
@@ -374,6 +404,21 @@
         match_count.reshape(1, 1),
         wall_geom,
     )
+    advanced, log_stress = pl.pallas_call(
+        hand_over,
+        out_shape=(
+            jax.ShapeDtypeStruct(advanced.shape, F32),
+            jax.ShapeDtypeStruct(log_stress.shape, F32),
+        ),
+        in_specs=[hbm, hbm],
+        out_specs=(hbm, hbm),
+        scratch_shapes=[
+            pltpu.VMEM(advanced.shape, F32),
+            pltpu.VMEM(log_stress.shape, F32),
+            pltpu.SemaphoreType.DMA((4 * comps + 1,)),
+            pltpu.SemaphoreType.DMA((4 * comps + 1,)),
+        ],
+    )(advanced, log_stress)
     return advanced, log_stress.reshape(points)
 
 

time: 32.7 us -> 31.6 us (0.966)
  local copies, waits for them, and re-layouts: 3.33 us -> 0 us
  Pallas kernels: 27.9 us -> 30.1 us
    unnamed x4 -> x0, local copies, waits for them, and re-layouts: 3.33 us -> none
    pallas_call x0 -> x1, Pallas kernels: none -> 2.35 us  [local(): pl.pallas_call(hand_over, out_shape=(jax.ShapeDtypeStruct(advanced.shape,...]
where the time goes in v1:
time: 31.6 us; the launch traced here: 31.4 us
  Pallas kernels  30.1 us (95%)
  between operations  1.29 us (4%)
    pallas_call x1, Pallas kernels, local(): pl.pallas_call(functools.partial(kernel, n_region, n_blk, cap), out_shape...  27.7 us
    pallas_call x1, Pallas kernels, local(): pl.pallas_call(hand_over, out_shape=(jax.ShapeDtypeStruct(advanced.shape,...  2.35 us

profile of v1, /device:TPU:0, one launch (start us, length us, event | category | flops | bytes accessed | tf_op | source)
XLA Modules:
  0.0 31.4 jit_solution(15606884445763692264)
XLA Ops:
  1.3 27.7 %shard_map.86 = (f32[3,16,32,256]{3,2,1,0:T(8,128)}, f32[8,128]{1,0:T(8,128)}) custom-call(f32[3,16,32,256]{3,2,1,0:T(8,128)} %v_hbm.1, f32[16,32,256]{2,1,0:T(8,128)} %visc_hbm.1, s32[1,1024]{1,0:T(1,128)} %bitcast.6, s32[1,1024]{1,0:T(1,128)} %bitcast.7, s32[1,1024]{1,0:T(1,128)} %bitcast.8, s32[1,1]{1,0:T(1,128)} %bitcast.5.count_ref, f32[4,2048]{1,0:T(4,128)} %geom_ref.1), custom_call_target="tpu_custom_call" | custom-call | tf_op jit(solution)/shard_map/pallas_call | solution.py:363
  29.0 2.4 %shard_map.87 = (f32[3,16,32,256]{3,2,1,0:T(8,128)}, f32[8,128]{1,0:T(8,128)}) custom-call(f32[3,16,32,256]{3,2,1,0:T(8,128)} %get-tuple-element.6.adv_in, f32[8,128]{1,0:T(8,128)} %get-tuple-element.7.log_in), custom_call_target="tpu_custom_call" | custom-call | tf_op jit(solution)/shard_map/pallas_call | solution.py:407
